TPU v7x, 512 devices: a whole 4x8x8 slice. The times are simulated.
512 devices in a mesh: seq: 128 (over y, z, core), fsdp: 4 (over x).
Axes of the slice: x: 4, y: 8, z: 8, core: 2. Of those that a mesh axis runs over, the one named last changes fastest.
Arguments:
- tokens: bfloat16 [4, 16384, 2048], P('fsdp', 'seq'), may hold values from -14 to 14
- w_qkv: bfloat16 [2048, 3, 1024], P(None, None, 'fsdp'), may hold values from -0.125 to 0.125
- w_feature: bfloat16 [8, 128, 16], replicated, may hold values from -2 to 2
- norm_gain: float32 [1024], replicated, may hold values from 0.5 to 1.5
- log_decay: float32 [4, 8, 16384], P('fsdp', None, 'seq'), may hold values from -1.5 to 0
- pattern: int32 [4, 256, 3], P('fsdp', 'seq'), may hold values from 1 to 255, as said below
Outputs:
- mixed: bfloat16 [4, 16384, 1024], P('fsdp', 'seq')
Inputs may be any that keep to these rules, and one draw needn't show every extreme that they name: `pattern`: the 3 blocks of query block b are distinct, none is among the first 1 block or equal to b - 1, b or b + 1, and each lies in a segment at most 3 segments from b's segment; the first lies exactly 3 segments later where that segment exists, else 3 segments earlier.
All inputs are finite; a program needn't handle non-finite values.
Results may differ from a plain program's by a relative error of at most 0.0097.
The roundings to bfloat16 on the way count: a program that leaves them out, or rounds other values in their place, can miss the bound.
Values may be sent and summed in bfloat16 or wider, within the bound.
No kernel may reach another device: no remote copies, remote signals or barrier semaphores. Data moves between devices by JAX's collectives and lax.ppermute only.
A program may use at most 64 MiB of HBM per device.

v0:
```python
import jax
import jax.numpy as jnp
from jax import lax
from jax.sharding import PartitionSpec as P

HALF_HEADS = 8
DH = 128
F = 16
HD = 1024
BS = 64
G = 1
R = 3
RD = 3
TOK_DEV = 128
NB_DEV = 2
epsilon = 1e-06
masked_score = -1e30


def from_behind(value, axis, steps):
    count = lax.axis_size(axis)
    initial, last = (max(0, -steps), min(count, count - steps))
    return lax.ppermute(value, axis, [(source, source + steps) for source in range(initial, last)])


def spread(array, axis, root):
    mine = lax.axis_index(axis) == root
    return lax.psum(jnp.where(mine, array, jnp.zeros_like(array)), axis)


def entering(value, axis, join, neutral):
    count, mine = (lax.axis_size(axis), lax.axis_index(axis))
    pieces = jax.tree.map(lambda part: lax.all_gather(part, axis), value)
    running = jax.tree.map(
        lambda part, zero: jnp.full_like(part, 0) + jnp.asarray(zero, part.dtype), value, neutral
    )

    def lap(position, running):
        longer = join(running, jax.tree.map(lambda part: part[position], pieces))
        return jax.tree.map(lambda new, old: jnp.where(position < mine, new, old), longer, running)

    return lax.fori_loop(0, count - 1, lap, running)


def feature_map(projected_head, w_feature):
    logits = jnp.einsum(
        "thd,hdf->htf", projected_head, w_feature, preferred_element_type=jnp.float32
    )
    return jax.nn.softmax(logits, axis=-1).astype(jnp.bfloat16)


def combine_states(earlier, following):
    return (earlier[0] * following[0], following[0][:, None, None] * earlier[1] + following[1])


def neighbour_piece(pair_rows, offset):
    return from_behind(pair_rows, "seq", -offset)


def per_device(tokens, w_qkv, w_feature, norm_gain, log_decay, pattern):
    projected = jnp.einsum(
        "btd,dkc->btkc",
        tokens,
        lax.all_gather(w_qkv, "fsdp", axis=2, tiled=True),
        preferred_element_type=jnp.float32,
    ).astype(jnp.bfloat16)
    queries = projected[0, :, 0].reshape(TOK_DEV, HALF_HEADS, DH)
    key_rows = projected[0, :, 1].reshape(TOK_DEV, HALF_HEADS, DH)
    values = projected[0, :, 2].reshape(TOK_DEV, HALF_HEADS, DH)
    pair_rows = projected[:, :, 1:3].reshape(1, TOK_DEV, 2 * HD)
    pieces = []
    for offset in range(-RD, RD + 1):
        if offset == 0:
            pieces.append(pair_rows)
        else:
            pieces.append(neighbour_piece(pair_rows, offset))
    region = jnp.concatenate(pieces, axis=1)
    global_rows = spread(pair_rows[0, : G * BS], "seq", 0)
    phi_query = feature_map(queries, w_feature)
    phi_key = feature_map(key_rows, w_feature)
    log_steps = log_decay[0]
    cumulative = jnp.cumsum(log_steps, axis=1)
    final_log = cumulative[:, -1:]
    weighted_key = (
        jnp.exp(final_log - cumulative)[:, :, None] * phi_key.astype(jnp.float32)
    ).astype(jnp.bfloat16)
    local_state = jnp.einsum(
        "htf,thd->hfd", weighted_key, values, preferred_element_type=jnp.float32
    )
    identity = (jnp.ones((HALF_HEADS,), jnp.float32), jnp.zeros((HALF_HEADS, F, DH), jnp.float32))
    carried_pair = entering(
        (jnp.exp(final_log[:, 0]), local_state), "seq", combine_states, identity
    )
    carried = carried_pair[1]
    scores = jnp.einsum("htf,hsf->hts", phi_query, phi_key, preferred_element_type=jnp.float32)
    log_gap = cumulative[:, :, None] - cumulative[:, None, :]
    causal = jnp.arange(TOK_DEV)[:, None] >= jnp.arange(TOK_DEV)[None, :]
    decay_matrix = jnp.where(causal[None], jnp.exp(jnp.minimum(log_gap, 0.0)), 0.0)
    mixing = (scores * decay_matrix).astype(jnp.bfloat16)
    local_term = jnp.einsum("hts,shd->thd", mixing, values, preferred_element_type=jnp.float32)
    carried_term = jnp.einsum(
        "htf,hfd->thd", phi_query.astype(jnp.float32), carried, precision=lax.Precision.HIGHEST
    )
    carried_term = carried_term * jnp.exp(cumulative).T[:, :, None]
    linear = local_term + carried_term
    normed = linear * lax.rsqrt(jnp.mean(linear * linear, axis=-1, keepdims=True) + epsilon)
    normed = normed * norm_gain.reshape(HALF_HEADS, DH)
    device = lax.axis_index("seq")
    block_total = lax.axis_size("seq") * NB_DEV
    window_blocks = region[0].reshape((2 * RD + 1) * NB_DEV, BS, 2 * HD)
    query_blocks = device * NB_DEV + jnp.arange(NB_DEV, dtype=jnp.int32)
    near_blocks = query_blocks[:, None] + jnp.arange(-1, 2, dtype=jnp.int32)[None, :]
    usable_near = (near_blocks >= G) & (near_blocks < block_total)
    chosen = jnp.concatenate([near_blocks, pattern[0]], axis=1) - (device - RD) * NB_DEV
    chosen = jnp.clip(chosen, 0, (2 * RD + 1) * NB_DEV - 1)
    usable = jnp.concatenate([usable_near, jnp.ones((NB_DEV, R), dtype=bool)], axis=1)
    usable_keys = jnp.repeat(usable, BS, axis=1)
    picked = jnp.take(window_blocks, chosen, axis=0).reshape(
        NB_DEV, (3 + R) * BS, 2, HALF_HEADS, DH
    )
    global_split = global_rows.reshape(G * BS, 2, HALF_HEADS, DH)
    query_rows = queries.reshape(NB_DEV, BS, HALF_HEADS, DH)
    score_scale = DH ** (-0.5)
    near_scores = (
        jnp.einsum(
            "nqhd,nkhd->nhqk", query_rows, picked[:, :, 0], preferred_element_type=jnp.float32
        )
        * score_scale
    )
    near_scores = jnp.where(usable_keys[:, None, None, :], near_scores, masked_score)
    far_scores = (
        jnp.einsum(
            "nqhd,khd->nhqk", query_rows, global_split[:, 0], preferred_element_type=jnp.float32
        )
        * score_scale
    )
    scores_all = jnp.concatenate([near_scores, far_scores], axis=-1)
    highest = jnp.max(scores_all, axis=-1, keepdims=True)
    exponent = jnp.exp(scores_all - highest)
    denominator = jnp.sum(exponent, axis=-1, keepdims=True)
    soft_weights = (exponent / denominator).astype(jnp.bfloat16)
    near_count = (3 + R) * BS
    sparse = jnp.einsum(
        "nhqk,nkhd->nqhd",
        soft_weights[..., :near_count],
        picked[:, :, 1],
        preferred_element_type=jnp.float32,
    )
    sparse = sparse + jnp.einsum(
        "nhqk,khd->nqhd",
        soft_weights[..., near_count:],
        global_split[:, 1],
        preferred_element_type=jnp.float32,
    )
    sparse = sparse.reshape(TOK_DEV, HALF_HEADS, DH)
    return (normed + sparse).astype(jnp.bfloat16).reshape(1, TOK_DEV, HD)


def solution(mesh):
    placed = (
        P("fsdp", "seq", None),
        P(None, None, "fsdp"),
        P(),
        P(),
        P("fsdp", None, "seq"),
        P("fsdp", "seq", None),
    )
    return jax.shard_map(
        per_device, mesh=mesh, in_specs=placed, out_specs=P("fsdp", "seq", None), check_vma=False
    )
```

profile of v0, /device:TPU:9, one launch (start us, length us, event | category | flops | bytes accessed | tf_op | source)
XLA Modules:
  0.0 615.5 jit_solution(8857086100503208488)
XLA Ops:
  7.9 133.5 %all-gather.5.cloned.1.call-done = bf16[2048,3,1024]{2,0,1:T(8,128)(2,1)} async-done(((bf16[2048,3,256]{2,0,1:T(8,128)(2,1)}), bf16[2048,3,1024]{2,0,1:T(8,128)(2,1)}) %all-gather.5.cloned.1.call-update) | async-done | bytes 12582928 | tf_op jit(solution)/shard_map/all_gather | solution.py:64
  141.4 6.4 %fusion.7 = bf16[1,128,3,1024]{3,1,2,0:T(8,128)(2,1)S(1)} fusion(bf16[2048,3,1024]{2,0,1:T(8,128)(2,1)} %all-gather.5.cloned.1.call-done, bf16[1,128,2048]{2,1,0:T(8,128)(2,1)S(1)} %copy-done), kind=kOutput, calls=%fused_computation.17 | convolution fusion | flops 1611005952 | bytes 13893632 | tf_op jit(solution)/shard_map/btd,dkc->btkc/dot_general | solution.py:61
  151.9 1.3 dynamic-slice
  154.0 213.7 %all-reduce.1 = f32[1024]{0:T(1024)S(1)} all-reduce(f32[1024]{0:T(1024)S(1)} %dynamic-update-slice), channel_id=2, replica_groups=mesh['seq'=128,'fsdp'=4] {'seq'}, use_global_device_ids=true, to_apply=%add.1 | all-reduce | flops 1024 | bytes 8192
  368.4 1.9 collective-permute-start
  370.3 1.9 collective-permute-start.1
  372.3 2.1 collective-permute-start.2
  374.3 5.9 collective-permute-start.3
  380.2 7.2 %collective-permute-start.4 = (bf16[1,128,2048]{1,2,0:T(8,128)(2,1)S(1)}, bf16[1,128,2048]{1,2,0:T(8,128)(2,1)S(1)}, u32[]{:S(2)}, u32[]{:S(2)}) collective-permute-start(bf16[1,128,2048]{1,2,0:T(8,128)(2,1)S(1)} %bitcast.123), channel_id=1, source_target_pairs={{8,0},{12,4},{16,8},{20,12},{24,16},{28,20},{32,24},{36,28},{40,32... | collective-permute-start | bytes 1572872 | tf_op jit(solution)/shard_map/ppermute | solution.py:23
  388.0 1.1 fusion.37
  389.4 8.5 %collective-permute-done = bf16[1,128,2048]{1,2,0:T(8,128)(2,1)} collective-permute-done((bf16[1,128,2048]{1,2,0:T(8,128)(2,1)S(1)}, bf16[1,128,2048]{1,2,0:T(8,128)(2,1)}, u32[]{:S(2)}, u32[]{:S(2)}) %collective-permute-start) | collective-permute-done | bytes 524320 | tf_op jit(solution)/shard_map/ppermute | solution.py:23
  397.9 3.3 collective-permute-start.5
  401.2 1.9 constant_dynamic-update-slice_fusion.6
  403.1 1.9 constant_dynamic-update-slice_fusion.5
  405.4 1.9 constant_dynamic-update-slice_fusion.4
  408.2 1.0 constant_dynamic-update-slice_fusion.2
  410.1 3.3 collective-permute-done.5
  414.2 6.2 %copy.54 = bf16[1,896,2048]{2,1,0:T(8,128)(2,1)} copy(bf16[1,896,2048]{1,2,0:T(8,128)(2,1)} %constant_dynamic-update-slice_fusion) | data formatting | bytes 7340032 | tf_op jit(solution)/shard_map/concatenate | solution.py:77
  420.4 4.6 gather_fusion
  425.0 2.9 copy.70
  432.0 52.2 %all-gather.7.cloned.1.call-done = f32[1024,16,128]{2,1,0:T(8,128)} async-done(((f32[8,16,128]{2,1,0:T(8,128)}), f32[1024,16,128]{2,1,0:T(8,128)}) %all-gather.7.cloned.1.call-update) | async-done | bytes 8388624 | tf_op jit(solution)/shard_map/all_gather | solution.py:33
  484.2 122.4 %while.14 = (s32[]{:T(128)}, f32[8,16,128]{2,1,0:T(8,128)S(1)}, s32[]{:T(128)}, f32[128,8]{1,0:T(8,128)S(1)}, f32[128,8,16,128]{3,2,1,0:T(8,128)}, /*index=5*/s32[]{:T(128)}, s32[]{:T(128)}) while((s32[]{:T(128)}, f32[8,16,128]{2,1,0:T(8,128)S(1)}, s32[]{:T(128)}, f32[128,8]{1,0:T(8,128)S(1)}, f32[128,8,16,128]{3,2,1,0:T(8,128)}, ...), condition=%wide.region_6.7_spmd.clone, body=%wide.region_5.6_spmd.clone.sunk | while | flops 65540 | bytes 196809 | solution.py:42
  485.2 0.9 fusion.58
  486.1 0.9 fusion.58
  487.1 0.9 fusion.58
  488.1 0.9 fusion.58
  489.0 0.9 fusion.58
  491.0 0.9 fusion.58
  492.9 0.9 fusion.58
  493.8 0.9 fusion.58
  494.8 0.9 fusion.58
  495.8 0.9 fusion.58
  496.7 0.9 fusion.58
  497.7 0.9 fusion.58
  498.7 0.9 fusion.58
  499.6 0.9 fusion.58
  500.6 0.9 fusion.58
  501.6 0.9 fusion.58
  502.5 0.9 fusion.58
  503.5 0.9 fusion.58
  504.4 0.9 fusion.58
  505.4 0.9 fusion.58
  506.4 0.9 fusion.58
  507.3 0.9 fusion.58
  509.3 0.9 fusion.58
  511.2 0.9 fusion.58
  512.2 0.9 fusion.58
  513.1 0.9 fusion.58
  (317 shorter events, 110.7 us)
Async XLA Ops:
  6.5 134.9 %copy-start = (bf16[1,128,2048]{2,1,0:T(8,128)(2,1)S(1)}, bf16[1,128,2048]{2,1,0:T(8,128)(2,1)}, u32[]{:S(2)}) copy-start(bf16[1,128,2048]{2,1,0:T(8,128)(2,1)} %param.8) | copy-start | bytes 1572868
  6.5 0.8 copy-start.6
  6.5 134.9 %all-gather.5.cloned.1.call-start = ((), (), s32[]{:S(2)}) async-start(), calls=%async_computation | async-start | bytes 15728640 | tf_op jit(solution)/shard_map/all_gather | solution.py:64
  7.3 380.8 %all-reduce.4.cloned.1.call-start = ((), (), s32[]{:S(2)}) async-start(), calls=%async_computation.1 | async-start | bytes 524288 | tf_op jit(solution)/shard_map/psum | solution.py:28
  147.8 1.5 copy-start.7
  147.8 2.8 copy-start.5
  149.2 335.0 %all-gather.7.cloned.1.call-start = ((), (), s32[]{:S(2)}) async-start(), calls=%async_computation.2 | async-start | bytes 8454144 | tf_op jit(solution)/shard_map/all_gather | solution.py:33
  149.5 237.9 %copy-start.8 = (f32[8,128,16]{1,2,0:T(8,128)}, f32[8,128,16]{1,2,0:T(8,128)S(1)}, u32[]{:S(2)}) copy-start(f32[8,128,16]{1,2,0:T(8,128)S(1)} %fusion.26) | copy-start | bytes 196612
  149.6 0.9 copy-start.10
  368.4 29.5 %collective-permute-start = (bf16[1,128,2048]{1,2,0:T(8,128)(2,1)S(1)}, bf16[1,128,2048]{1,2,0:T(8,128)(2,1)}, u32[]{:S(2)}, u32[]{:S(2)}) collective-permute-start(bf16[1,128,2048]{1,2,0:T(8,128)(2,1)S(1)} %bitcast.119), channel_id=1, source_target_pairs={{0,12},{4,16},{8,20},{12,24},{16,28},{20,32},{24,36},{28,40},{32,4... | collective-permute-start | bytes 1572872 | tf_op jit(solution)/shard_map/ppermute | solution.py:23
  370.3 32.8 %collective-permute-start.1 = (bf16[1,128,2048]{1,2,0:T(8,128)(2,1)S(1)}, bf16[1,128,2048]{1,2,0:T(8,128)(2,1)}, u32[]{:S(2)}, u32[]{:S(2)}) collective-permute-start(bf16[1,128,2048]{1,2,0:T(8,128)(2,1)S(1)} %bitcast.120), channel_id=1, source_target_pairs={{0,8},{4,12},{8,16},{12,20},{16,24},{20,28},{24,32},{28,36},{32,40... | collective-permute-start | bytes 1572872 | tf_op jit(solution)/shard_map/ppermute | solution.py:23
  372.3 33.1 %collective-permute-start.2 = (bf16[1,128,2048]{1,2,0:T(8,128)(2,1)S(1)}, bf16[1,128,2048]{1,2,0:T(8,128)(2,1)}, u32[]{:S(2)}, u32[]{:S(2)}) collective-permute-start(bf16[1,128,2048]{1,2,0:T(8,128)(2,1)S(1)} %bitcast.121), channel_id=1, source_target_pairs={{0,4},{4,8},{8,12},{12,16},{16,20},{20,24},{24,28},{28,32},{32,36}... | collective-permute-start | bytes 1572872 | tf_op jit(solution)/shard_map/ppermute | solution.py:23
  374.3 33.8 %collective-permute-start.3 = (bf16[1,128,2048]{1,2,0:T(8,128)(2,1)S(1)}, bf16[1,128,2048]{1,2,0:T(8,128)(2,1)S(1)}, u32[]{:S(2)}, u32[]{:S(2)}) collective-permute-start(bf16[1,128,2048]{1,2,0:T(8,128)(2,1)S(1)} %bitcast.122), channel_id=1, source_target_pairs={{4,0},{8,4},{12,8},{16,12},{20,16},{24,20},{28,24},{32,28},{36,32}... | collective-permute-start | bytes 1572872 | tf_op jit(solution)/shard_map/ppermute | solution.py:23
  380.2 28.9 %collective-permute-start.4 = (bf16[1,128,2048]{1,2,0:T(8,128)(2,1)S(1)}, bf16[1,128,2048]{1,2,0:T(8,128)(2,1)S(1)}, u32[]{:S(2)}, u32[]{:S(2)}) collective-permute-start(bf16[1,128,2048]{1,2,0:T(8,128)(2,1)S(1)} %bitcast.123), channel_id=1, source_target_pairs={{8,0},{12,4},{16,8},{20,12},{24,16},{28,20},{32,24},{36,28},{40,32... | collective-permute-start | bytes 1572872 | tf_op jit(solution)/shard_map/ppermute | solution.py:23
  397.9 15.4 %collective-permute-start.5 = (bf16[1,128,2048]{1,2,0:T(8,128)(2,1)S(1)}, bf16[1,128,2048]{1,2,0:T(8,128)(2,1)S(1)}, u32[]{:S(2)}, u32[]{:S(2)}) collective-permute-start(bf16[1,128,2048]{1,2,0:T(8,128)(2,1)S(1)} %bitcast.124), channel_id=1, source_target_pairs={{12,0},{16,4},{20,8},{24,12},{28,16},{32,20},{36,24},{40,28},{44,3... | collective-permute-start | bytes 1572872 | tf_op jit(solution)/shard_map/ppermute | solution.py:23
  427.9 0.8 copy-start.3
  430.3 1.0 copy-start.1
  431.2 176.0 %copy-start.2 = (pred[128,128]{1,0:T(8,128)(4,1)S(1)}, pred[128,128]{1,0:T(8,128)(4,1)}, u32[]{:S(2)}) copy-start(pred[128,128]{1,0:T(8,128)(4,1)} %iota_compare_fusion) | copy-start | bytes 49156
  431.3 176.0 %copy-start.9 = (f32[8,128,16]{1,2,0:T(8,128)S(1)}, f32[8,128,16]{1,2,0:T(8,128)}, u32[]{:S(2)}) copy-start(f32[8,128,16]{1,2,0:T(8,128)} %copy-done.8) | copy-start | bytes 196612
  431.3 176.0 %copy-start.11 = (f32[8,128]{1,0:T(8,128)S(1)}, f32[8,128]{1,0:T(8,128)}, u32[]{:S(2)}) copy-start(f32[8,128]{1,0:T(8,128)} %copy-done.10) | copy-start | bytes 12292
  431.5 176.4 %copy-start.4 = (f32[1024]{0:T(1024)S(1)}, f32[1024]{0:T(1024)}, u32[]{:S(2)}) copy-start(f32[1024]{0:T(1024)} %param.11) | copy-start | bytes 12292
Sparse Core Ops, SparseCore 0:
  9.5 131.8 all-gather.4
  149.3 190.4 all-reduce.3
  342.9 141.2 all-gather.6
where the time goes:
time: 622 us; the launch traced here: 615 us
  blocking collectives  214 us (34%)
  waiting for transfers between devices  199 us (32%)
  other arithmetic  121 us (19%)
  local copies, waits for them, and re-layouts  30.1 us (5%)
  starting transfers between devices  22.4 us (4%)
  between operations  14.2 us (2%)
  matrix products  11.5 us (2%)
    unnamed x1, blocking collectives  214 us
    all_gather x1, waiting for transfers between devices, per_device(): lax.all_gather(w_qkv, 'fsdp', axis=2, tiled=True)  134 us
    select_n x127, other arithmetic, lap(): jnp.where(position < mine, new, old)  117 us
    all_gather x1, waiting for transfers between devices, entering(): pieces = jax.tree.map(lambda part: lax.all_gather(part, axis), value)  52.2 us
    ppermute x6, starting transfers between devices, from_behind(): lax.ppermute(value, axis, [(source, source + steps) for source in range(i...  22.3 us
    unnamed x38, local copies, waits for them, and re-layouts  13.2 us
  transfers between devices with their start and end apart: 9, of which 5 were waited for; matrix products, arithmetic and copies ran while one was open for 6% of the time, Pallas kernels for 0%

commit v1 on v0

--- a/solution.py
+++ b/solution.py
@@ -1,7 +1,9 @@
+import functools
 import jax
 import jax.numpy as jnp
 from jax import lax
 from jax.sharding import PartitionSpec as P
+from jax.lax import all_to_all, axis_size
 
 HALF_HEADS = 8
 DH = 128
@@ -15,6 +17,15 @@
 NB_DEV = 2
 epsilon = 1e-06
 masked_score = -1e30
+
+
+def state_name(obj, dim_i):
+    heard = jnp.stack([obj for _ in range(axis_size("fsdp"))])
+    u_next = all_to_all(heard, "fsdp", 0, 0)
+    return jnp.concatenate(u_next, axis=dim_i)
+
+
+recover_flows = functools.partial(state_name, dim_i=2)
 
 
 def from_behind(value, axis, steps):
@@ -59,10 +70,7 @@
 
 def per_device(tokens, w_qkv, w_feature, norm_gain, log_decay, pattern):
     projected = jnp.einsum(
-        "btd,dkc->btkc",
-        tokens,
-        lax.all_gather(w_qkv, "fsdp", axis=2, tiled=True),
-        preferred_element_type=jnp.float32,
+        "btd,dkc->btkc", tokens, recover_flows(w_qkv), preferred_element_type=jnp.float32
     ).astype(jnp.bfloat16)
     queries = projected[0, :, 0].reshape(TOK_DEV, HALF_HEADS, DH)
     key_rows = projected[0, :, 1].reshape(TOK_DEV, HALF_HEADS, DH)

time: 622 us -> 736 us (1.18)
  the two profiles are of different devices: /device:TPU:9 before, /device:TPU:32 now
where the time goes in v1:
time: 736 us; the launch traced here: 726 us
  blocking collectives  254 us (35%)
  waiting for transfers between devices  171 us (23%)
  local copies, waits for them, and re-layouts  131 us (18%)
  other arithmetic  120 us (16%)
  starting transfers between devices  25.3 us (3%)
  between operations  14.6 us (2%)
    unnamed x1, blocking collectives  254 us
    all_to_all x1, waiting for transfers between devices, state_name(): u_next = all_to_all(heard, 'fsdp', 0, 0)  138 us
    select_n x127, other arithmetic, lap(): jnp.where(position < mine, new, old)  117 us
    mul x127, local copies, waits for them, and re-layouts, combine_states(): following[0][:, None, None] * earlier[1] + following[1]  87.3 us
    ppermute x6, waiting for transfers between devices, from_behind(): lax.ppermute(value, axis, [(source, source + steps) for source in range(i...  32.1 us
    ppermute x6, starting transfers between devices, from_behind(): lax.ppermute(value, axis, [(source, source + steps) for source in range(i...  18.7 us
  transfers between devices with their start and end apart: 9, of which 6 were waited for; matrix products, arithmetic and copies ran while one was open for 5% of the time, Pallas kernels for 0%

profile of v1, /device:TPU:32, one launch (start us, length us, event | category | flops | bytes accessed | tf_op | source)
XLA Modules:
  0.0 725.6 jit_solution(2145646538984858502)
XLA Ops:
  6.5 7.5 %stack.2 = bf16[4,2048,3,256]{3,1,2,0:T(8,128)(2,1)} broadcast(bf16[2048,3,256]{2,0,1:T(8,128)(2,1)} %param.9), dimensions={1,2,3} | broadcast | bytes 15728640 | tf_op jit(solution)/shard_map/stack | solution.py:23
  14.0 6.5 all-to-all-start
  21.1 138.4 %all-to-all-done = bf16[4,2048,3,256]{3,1,2,0:T(8,128)(2,1)} async-done(((bf16[4,2048,3,256]{3,1,2,0:T(8,128)(2,1)}), bf16[4,2048,3,256]{3,1,2,0:T(8,128)(2,1)}, u32[]{:S(2)}, u32[]{:S(2)}) %all-to-all-start) | async-done | bytes 12582944 | tf_op jit(solution)/shard_map/all_to_all | solution.py:24
  159.5 6.6 copy.67
  166.1 1.8 fusion.7
  172.5 1.3 dynamic-slice
  174.8 254.4 %all-reduce.1 = f32[1024]{0:T(1024)S(1)} all-reduce(f32[1024]{0:T(1024)S(1)} %dynamic-update-slice), channel_id=2, replica_groups=mesh['seq'=128,'fsdp'=4] {'seq'}, use_global_device_ids=true, to_apply=%add.1 | all-reduce | flops 1024 | bytes 8192
  430.5 1.9 collective-permute-start
  432.4 1.9 collective-permute-start.1
  434.4 1.9 collective-permute-start.2
  436.3 7.0 collective-permute-start.3
  443.3 3.9 collective-permute-start.4
  448.2 1.1 fusion.37
  449.6 1.7 collective-permute-done
  451.3 2.1 collective-permute-start.5
  453.4 1.9 constant_dynamic-update-slice_fusion.6
  455.3 8.1 %collective-permute-done.1 = bf16[1,128,2048]{1,2,0:T(8,128)(2,1)} collective-permute-done((bf16[1,128,2048]{1,2,0:T(8,128)(2,1)S(1)}, bf16[1,128,2048]{1,2,0:T(8,128)(2,1)}, u32[]{:S(2)}, u32[]{:S(2)}) %collective-permute-start.1) | collective-permute-done | bytes 524320 | tf_op jit(solution)/shard_map/ppermute | solution.py:34
  463.3 1.9 constant_dynamic-update-slice_fusion.5
  465.3 3.0 collective-permute-done.2
  470.0 1.0 constant_dynamic-update-slice_fusion.2
  471.0 1.8 collective-permute-done.4
  473.8 17.5 %collective-permute-done.5 = bf16[1,128,2048]{1,2,0:T(8,128)(2,1)S(1)} collective-permute-done((bf16[1,128,2048]{1,2,0:T(8,128)(2,1)S(1)}, bf16[1,128,2048]{1,2,0:T(8,128)(2,1)S(1)}, u32[]{:S(2)}, u32[]{:S(2)}) %collective-permute-start.5) | collective-permute-done | bytes 524320 | tf_op jit(solution)/shard_map/ppermute | solution.py:34
  492.2 6.2 copy.55
  498.4 4.7 gather_fusion
  503.1 2.9 copy.72
  510.1 206.2 %while.14 = (s32[]{:T(128)}, f32[8,16,128]{2,1,0:T(8,128)S(1)}, s32[]{:T(128)}, f32[128,8]{1,0:T(8,128)}, f32[128,8,16,128]{3,2,1,0:T(8,128)}, /*index=5*/s32[]{:T(128)}, s32[]{:T(128)}) while((s32[]{:T(128)}, f32[8,16,128]{2,1,0:T(8,128)S(1)}, s32[]{:T(128)}, f32[128,8]{1,0:T(8,128)}, f32[128,8,16,128]{3,2,1,0:T(8,128)}, ...), condition=%wide.region_6.7_spmd.clone, body=%wide.region_5.6_spmd.clone.sunk | while | flops 65540 | bytes 196809 | solution.py:53
  510.9 0.9 fusion.58
  514.1 0.9 fusion.58
  515.8 0.9 fusion.58
  519.0 0.9 fusion.58
  523.9 0.9 fusion.58
  525.5 0.9 fusion.58
  527.1 0.9 fusion.58
  535.3 0.9 fusion.58
  536.9 0.9 fusion.58
  541.7 0.9 fusion.58
  548.2 0.9 fusion.58
  553.1 0.9 fusion.58
  557.9 0.9 fusion.58
  562.8 0.9 fusion.58
  564.4 0.9 fusion.58
  567.6 0.9 fusion.58
  569.3 0.9 fusion.58
  574.1 0.9 fusion.58
  575.7 0.9 fusion.58
  577.4 0.9 fusion.58
  579.0 0.9 fusion.58
  580.6 0.9 fusion.58
  (326 shorter events, 201.2 us)
Async XLA Ops:
  6.5 159.6 %copy-start = (bf16[1,128,2048]{2,1,0:T(8,128)(2,1)S(1)}, bf16[1,128,2048]{2,1,0:T(8,128)(2,1)}, u32[]{:S(2)}) copy-start(bf16[1,128,2048]{2,1,0:T(8,128)(2,1)} %param.8) | copy-start | bytes 1572868
  14.0 6.5 copy-start.10
  14.0 145.5 %all-to-all-start = ((bf16[4,2048,3,256]{3,1,2,0:T(8,128)(2,1)}), bf16[4,2048,3,256]{3,1,2,0:T(8,128)(2,1)}, u32[]{:S(2)}, u32[]{:S(2)}) async-start(bf16[4,2048,3,256]{3,1,2,0:T(8,128)(2,1)} %stack.2), calls=%async_computation | async-start | bytes 25165824 | tf_op jit(solution)/shard_map/all_to_all | solution.py:24
  20.5 427.3 %all-reduce.4.cloned.1.call-start = ((), (), s32[]{:S(2)}) async-start(), calls=%async_computation.1 | async-start | bytes 524288 | tf_op jit(solution)/shard_map/psum | solution.py:39
  167.9 1.5 copy-start.11
  168.0 2.7 copy-start.9
  169.3 340.8 %all-gather.4.cloned.1.call-start = ((), (), s32[]{:S(2)}) async-start(), calls=%async_computation.2 | async-start | bytes 8454144 | tf_op jit(solution)/shard_map/all_gather | solution.py:44
  169.7 277.6 %copy-start.12 = (f32[8,128,16]{1,2,0:T(8,128)}, f32[8,128,16]{1,2,0:T(8,128)S(1)}, u32[]{:S(2)}) copy-start(f32[8,128,16]{1,2,0:T(8,128)S(1)} %fusion.26) | copy-start | bytes 196612
  169.7 1.2 copy-start.14
  430.5 20.8 %collective-permute-start = (bf16[1,128,2048]{1,2,0:T(8,128)(2,1)S(1)}, bf16[1,128,2048]{1,2,0:T(8,128)(2,1)}, u32[]{:S(2)}, u32[]{:S(2)}) collective-permute-start(bf16[1,128,2048]{1,2,0:T(8,128)(2,1)S(1)} %bitcast.123), channel_id=1, source_target_pairs={{0,12},{4,16},{8,20},{12,24},{16,28},{20,32},{24,36},{28,40},{32,4... | collective-permute-start | bytes 1572872 | tf_op jit(solution)/shard_map/ppermute | solution.py:34
  432.4 30.9 %collective-permute-start.1 = (bf16[1,128,2048]{1,2,0:T(8,128)(2,1)S(1)}, bf16[1,128,2048]{1,2,0:T(8,128)(2,1)}, u32[]{:S(2)}, u32[]{:S(2)}) collective-permute-start(bf16[1,128,2048]{1,2,0:T(8,128)(2,1)S(1)} %bitcast.124), channel_id=1, source_target_pairs={{0,8},{4,12},{8,16},{12,20},{16,24},{20,28},{24,32},{28,36},{32,40... | collective-permute-start | bytes 1572872 | tf_op jit(solution)/shard_map/ppermute | solution.py:34
  434.4 33.9 %collective-permute-start.2 = (bf16[1,128,2048]{1,2,0:T(8,128)(2,1)S(1)}, bf16[1,128,2048]{1,2,0:T(8,128)(2,1)S(1)}, u32[]{:S(2)}, u32[]{:S(2)}) collective-permute-start(bf16[1,128,2048]{1,2,0:T(8,128)(2,1)S(1)} %bitcast.125), channel_id=1, source_target_pairs={{0,4},{4,8},{8,12},{12,16},{16,20},{20,24},{24,28},{28,32},{32,36}... | collective-permute-start | bytes 1572872 | tf_op jit(solution)/shard_map/ppermute | solution.py:34
  436.3 33.7 %collective-permute-start.3 = (bf16[1,128,2048]{1,2,0:T(8,128)(2,1)S(1)}, bf16[1,128,2048]{1,2,0:T(8,128)(2,1)S(1)}, u32[]{:S(2)}, u32[]{:S(2)}) collective-permute-start(bf16[1,128,2048]{1,2,0:T(8,128)(2,1)S(1)} %bitcast.126), channel_id=1, source_target_pairs={{4,0},{8,4},{12,8},{16,12},{20,16},{24,20},{28,24},{32,28},{36,32}... | collective-permute-start | bytes 1572872 | tf_op jit(solution)/shard_map/ppermute | solution.py:34
  443.3 29.6 %collective-permute-start.4 = (bf16[1,128,2048]{1,2,0:T(8,128)(2,1)S(1)}, bf16[1,128,2048]{1,2,0:T(8,128)(2,1)S(1)}, u32[]{:S(2)}, u32[]{:S(2)}) collective-permute-start(bf16[1,128,2048]{1,2,0:T(8,128)(2,1)S(1)} %bitcast.127), channel_id=1, source_target_pairs={{8,0},{12,4},{16,8},{20,12},{24,16},{28,20},{32,24},{36,28},{40,32... | collective-permute-start | bytes 1572872 | tf_op jit(solution)/shard_map/ppermute | solution.py:34
  447.5 0.7 copy-start.3
  451.3 40.0 %collective-permute-start.5 = (bf16[1,128,2048]{1,2,0:T(8,128)(2,1)S(1)}, bf16[1,128,2048]{1,2,0:T(8,128)(2,1)S(1)}, u32[]{:S(2)}, u32[]{:S(2)}) collective-permute-start(bf16[1,128,2048]{1,2,0:T(8,128)(2,1)S(1)} %bitcast.128), channel_id=1, source_target_pairs={{12,0},{16,4},{20,8},{24,12},{28,16},{32,20},{36,24},{40,28},{44,3... | collective-permute-start | bytes 1572872 | tf_op jit(solution)/shard_map/ppermute | solution.py:34
  503.1 2.9 copy-start.6
  506.0 0.8 copy-start.7
  508.4 1.0 copy-start.2
  509.3 207.7 %copy-start.4 = (f32[8,128,16]{1,2,0:T(8,128)S(1)}, f32[8,128,16]{1,2,0:T(8,128)}, u32[]{:S(2)}) copy-start(f32[8,128,16]{1,2,0:T(8,128)} %copy-done.3) | copy-start | bytes 196612
  509.3 207.7 %copy-start.5 = (pred[128,128]{1,0:T(8,128)(4,1)S(1)}, pred[128,128]{1,0:T(8,128)(4,1)}, u32[]{:S(2)}) copy-start(pred[128,128]{1,0:T(8,128)(4,1)} %iota_compare_fusion) | copy-start | bytes 49156
  509.3 207.7 %copy-start.13 = (f32[8,128,16]{1,2,0:T(8,128)S(1)}, f32[8,128,16]{1,2,0:T(8,128)}, u32[]{:S(2)}) copy-start(f32[8,128,16]{1,2,0:T(8,128)} %copy-done.12) | copy-start | bytes 196612
  509.3 207.7 %copy-start.15 = (f32[8,128]{1,0:T(8,128)S(1)}, f32[8,128]{1,0:T(8,128)}, u32[]{:S(2)}) copy-start(f32[8,128]{1,0:T(8,128)} %copy-done.14) | copy-start | bytes 12292
  509.5 208.1 %copy-start.8 = (f32[1024]{0:T(1024)S(1)}, f32[1024]{0:T(1024)}, u32[]{:S(2)}) copy-start(f32[1024]{0:T(1024)} %param.11) | copy-start | bytes 12292
  509.9 208.9 %copy-start.1 = (bf16[1,128,2048]{2,1,0:T(8,128)(2,1)S(1)}, bf16[1,128,2048]{2,1,0:T(8,128)(2,1)}, u32[]{:S(2)}) copy-start(bf16[1,128,2048]{2,1,0:T(8,128)(2,1)} %param.8) | copy-start | bytes 1572868
Sparse Core Ops, SparseCore 0:
  169.4 190.5 all-reduce.3
  363.2 141.1 all-gather.3
